TPU v7x, 32 devices: a whole 2x2x4 slice. The times are simulated.
32 devices in a mesh: rows: 8 (over z, y), grp: 4 (over x, core).
Axes of the slice: x: 2, y: 2, z: 4, core: 2. Of those that a mesh axis runs over, the one named last changes fastest.
Arguments:
- tiles: float32 [1536, 128, 128], P(('rows', 'grp')), may hold values from 0 to 24
- coords: int32 [1536, 2], P(('rows', 'grp')), may hold values from 0 to 127, as said below
- live: int32 [32], P(('rows', 'grp')), may hold values from 6 to 48, as said below
- sketch: float32 [16384, 64], P(('rows', 'grp')), may hold values from -6 to 6
Outputs:
- basis: float32 [16384, 64], P(('rows', 'grp'))
Inputs may be any that keep to these rules, and one draw needn't show every extreme that they name: `coords`: slot s of device d (slot d * 48 + s) has the row tile d * 4 + s and the column tile equal to it for s < 4; every other slot of device d has a row tile from d * 4 to d * 4 + 3, and a column tile in row block b - 1, b or b + 1 (modulo 8), where b = d // 4 and row block b is the tiles b * 16 to b * 16 + 15; slot 4 has its column tile in row block b - 1 and slot 5 in row block b + 1. The same coordinate pair may repeat. `live`: every device uses its slots 4 and 5; some device uses all 48.
All inputs are finite; a program needn't handle non-finite values.
Results may differ from a plain program's by a relative error of at most 0.0003.
Values sent between devices are 32-bit elements; how exact they have to be, the bound alone decides.
A program may use at most 64 MiB of HBM per device.

v0:
```python
import jax
import jax.numpy as jnp
from jax import lax
from jax.sharding import PartitionSpec as P

HIGHEST = lax.Precision.HIGHEST


def from_behind(array, axis, by):
    peers = lax.axis_size(axis)
    return lax.ppermute(array, axis, [(i, (i + by) % peers) for i in range(peers)])


def padded(cells, sides, width):
    for axis, dim in sides:
        count = lax.axis_size(axis)
        head = lax.slice_in_dim(cells, 0, width, axis=dim)
        tail = lax.slice_in_dim(cells, cells.shape[dim] - width, cells.shape[dim], axis=dim)
        cells = jnp.concatenate(
            [
                lax.ppermute(tail, axis, [(i, (i + 1) % count) for i in range(count)]),
                cells,
                lax.ppermute(head, axis, [((i + 1) % count, i) for i in range(count)]),
            ],
            axis=dim,
        )
    return cells


def product_sweep(tile_slab, live_count, source, source_pos, target_pos, targets, transpose):
    target_ids = jnp.arange(targets, dtype=jnp.int32)
    lane_ids = jnp.arange(8, dtype=jnp.int32)
    initial = jnp.zeros((targets, source.shape[1], source.shape[2]), jnp.float32)
    pattern = "sji,sjk->sik" if transpose else "sij,sjk->sik"

    def advance(number, summed):
        offset = number * 8
        stacked = lax.dynamic_slice_in_dim(tile_slab, offset, 8, 0)
        fetched = lax.dynamic_slice_in_dim(source_pos, offset, 8, 0)
        placed = lax.dynamic_slice_in_dim(target_pos, offset, 8, 0)
        product = jnp.einsum(pattern, stacked, source[fetched], precision=HIGHEST)
        active = offset + lane_ids < live_count
        selector = ((placed[None, :] == target_ids[:, None]) & active[None, :]).astype(jnp.float32)
        return summed + jnp.einsum("ns,sik->nik", selector, product, precision=HIGHEST)

    return lax.fori_loop(0, (live_count + 7) // 8, advance, initial)


def local(tiles, coords, live, sketch):
    groups = lax.axis_size("grp")
    cycle_size = lax.axis_size("rows")
    row_index = lax.axis_index("rows")
    grp_index = lax.axis_index("grp")
    tile_edge = tiles.shape[1]
    columns = sketch.shape[1]
    per_device = sketch.shape[0] // tile_edge
    block_tiles = groups * per_device
    block_base = row_index * block_tiles
    own_base = block_base + grp_index * per_device
    row_pos = coords[:, 0] - own_base
    live_count = live[0]
    col_tiles = coords[:, 1]
    span_pos = (
        col_tiles // block_tiles - row_index + 1 + cycle_size
    ) % cycle_size * block_tiles + col_tiles % block_tiles
    panel = sketch
    for sweep in range(2):
        panel_rows = panel
        source = panel_rows.reshape(-1, tile_edge, columns)
        spread = product_sweep(tiles, live_count, source, row_pos, span_pos, 3 * block_tiles, True)
        spread = spread.reshape(3, block_tiles * tile_edge, columns)
        from_next = from_behind(spread[0], "rows", -1)
        from_prior = from_behind(spread[2], "rows", 1)
        summed = spread[1] + from_next + from_prior
        middle_rows = lax.psum_scatter(summed, "grp", scatter_dimension=0, tiled=True)
        whole = lax.all_gather(middle_rows, "grp", axis=0, tiled=True)
        widened = padded(whole, (("rows", 0),), whole.shape[0])
        source = widened.reshape(-1, tile_edge, columns)
        image = product_sweep(tiles, live_count, source, span_pos, row_pos, per_device, False)
        image = image.reshape(-1, columns)
        gram = lax.psum(
            jnp.dot(image.T, image, precision=HIGHEST, preferred_element_type=jnp.float32),
            ("rows", "grp"),
        )
        lower = jnp.linalg.cholesky(gram)
        panel = jax.scipy.linalg.solve_triangular(lower, image.T, lower=True).T
    total_rows = cycle_size * groups * sketch.shape[0]
    return panel * total_rows**0.5


def solution(mesh):
    return jax.shard_map(
        local,
        mesh=mesh,
        in_specs=(
            P(("rows", "grp"), None, None),
            P(("rows", "grp"), None),
            P(("rows", "grp")),
            P(("rows", "grp"), None),
        ),
        out_specs=P(("rows", "grp"), None),
        check_vma=False,
    )
```

profile of v0, /device:TPU:0, one launch (start us, length us, event | category | flops | bytes accessed | tf_op | source)
XLA Modules:
  0.0 396.6 jit_solution(9603917095713497614)
XLA Ops:
  7.2 0.7 fusion.71
  7.9 0.7 subtract_bitcast_fusion
  8.6 1.0 copy.21
  9.8 4.8 %while.44 = (s32[]{:T(128)}, f32[48,128,64]{1,0,2:T(8,128)S(1)}, s32[]{:T(128)}, s32[48]{0:T(128)S(1)}, s32[]{:T(128)}, /*index=5*/f32[48,128,128]{2,1,0:T(8,128...) while((s32[]{:T(128)}, f32[48,128,64]{1,0,2:T(8,128)S(1)}, ...), condition=%wide.region_1.2_spmd.clone, body=%wide.region_0.1_spmd.clone.sunk | while | flops 138807088 | bytes 4985255 | solution.py:46
  10.5 2.0 fusion.108
  13.3 1.3 convolution_add_fusion.8
  14.9 15.7 %collective-permute-start = (f32[2048,64]{0,1:T(8,128)S(1)}, f32[2048,64]{0,1:T(8,128)S(1)}, u32[]{:S(2)}, u32[]{:S(2)}) collective-permute-start(f32[2048,64]{0,1:T(8,128)S(1)} %bitcast.147), channel_id=1, source_target_pairs={{0,28},{4,0},{8,4},{12,8},{16,12},{20,16},{24,20},{28,24},{1,29},{... | collective-permute-start | bytes 1572872 | tf_op jit(solution)/shard_map/ppermute | solution.py:11
  30.8 6.7 %collective-permute-start.1 = (f32[2048,64]{0,1:T(8,128)S(1)}, f32[2048,64]{0,1:T(8,128)S(1)}, u32[]{:S(2)}, u32[]{:S(2)}) collective-permute-start(f32[2048,64]{0,1:T(8,128)S(1)} %bitcast.149), channel_id=1, source_target_pairs={{0,4},{4,8},{8,12},{12,16},{16,20},{20,24},{24,28},{28,0},{1,5},{5... | collective-permute-start | bytes 1572872 | tf_op jit(solution)/shard_map/ppermute | solution.py:11
  37.4 12.5 %collective-permute-done = f32[2048,64]{0,1:T(8,128)S(1)} collective-permute-done((f32[2048,64]{0,1:T(8,128)S(1)}, f32[2048,64]{0,1:T(8,128)S(1)}, u32[]{:S(2)}, u32[]{:S(2)}) %collective-permute-start) | collective-permute-done | bytes 524320 | tf_op jit(solution)/shard_map/ppermute | solution.py:11
  50.0 5.1 %collective-permute-done.1 = f32[2048,64]{0,1:T(8,128)S(1)} collective-permute-done((f32[2048,64]{0,1:T(8,128)S(1)}, f32[2048,64]{0,1:T(8,128)S(1)}, u32[]{:S(2)}, u32[]{:S(2)}) %collective-permute-start.1) | collective-permute-done | bytes 524320 | tf_op jit(solution)/shard_map/ppermute | solution.py:11
  55.0 1.0 fusion.58
  56.1 23.0 %reduce-scatter.3.cloned.1.call-done = f32[512,64]{0,1:T(8,128)} async-done(((f32[2048,64]{0,1:T(8,128)}), f32[512,64]{0,1:T(8,128)}) %reduce-scatter.3.cloned.1.call-update) | async-done | bytes 131088 | tf_op jit(solution)/shard_map/reduce_scatter | solution.py:75
  79.1 7.0 %all_gather.6 = f32[2048,64]{0,1:T(8,128)S(1)} all-gather(f32[512,64]{0,1:T(8,128)} %reduce-scatter.3.cloned.1.call-done), channel_id=1, replica_groups=mesh['rows'=8,'grp'=4] {'grp'}, dimensions={0}, use_global_device_ids=true | all-gather | bytes 655360 | tf_op jit(solution)/shard_map/all_gather | solution.py:76
  86.1 1.5 collective-permute-start.2
  87.5 3.2 collective-permute-start.3
  90.8 19.7 %collective-permute-done.2 = f32[2048,64]{0,1:T(8,128)S(1)} collective-permute-done((f32[2048,64]{0,1:T(8,128)S(1)}, f32[2048,64]{0,1:T(8,128)S(1)}, u32[]{:S(2)}, u32[]{:S(2)}) %collective-permute-start.2) | collective-permute-done | bytes 524320 | tf_op jit(solution)/shard_map/ppermute | solution.py:21
  110.5 2.2 collective-permute-done.3
  112.8 2.3 copy.39
  115.1 6.0 %while.45 = (s32[]{:T(128)}, f32[4,128,64]{1,0,2:T(4,128)S(1)}, s32[]{:T(128)}, s32[48]{0:T(128)S(1)}, s32[]{:T(128)}, /*index=5*/f32[48,128,128]{2,1,0:T(8,128)...) while((s32[]{:T(128)}, f32[4,128,64]{1,0,2:T(4,128)S(1)}, ...), condition=%wide.region_4.5_spmd.clone, body=%wide.region_3.4_spmd.clone.sunk | while | flops 103842928 | bytes 2101671 | solution.py:46
  115.2 2.5 gather_fusion.1
  117.7 2.1 fusion.114
  121.3 67.8 %psum.14 = f32[64,64]{0,1:T(8,128)S(1)} all-reduce(f32[64,64]{0,1:T(8,128)S(1)} %convolution_bitcast_fusion.2), channel_id=1, replica_groups=mesh['rows'=8,'grp'=4] {'rows','grp'}, use_global_device_ids=true, to_apply=%region_5.6 | all-reduce | flops 4096 | bytes 32768 | tf_op jit(solution)/shard_map/psum | solution.py:81
  189.2 5.8 %cholesky.44 = f32[64,64]{1,0:T(8,128)S(1)} custom-call(f32[64,64]{1,0:T(8,128)S(1)} %fusion.68), custom_call_target="Cholesky" | custom-call | tf_op jit(solution)/shard_map/jit(cholesky)/cholesky | solution.py:85
  195.1 0.7 compare_reduce_fusion.1
  195.8 0.7 fusion.63
  196.5 4.9 %custom-call.6 = f32[1,64,64]{1,2,0:T(8,128)S(1)} custom-call(f32[1,64,64]{2,1,0:T(8,128)S(1)} %fusion.63), custom_call_target="InvertDiagBlocksLowerTriangular" | custom-call | tf_op jit(solution)/shard_map/jit(_solve_triangular)/triangular_solve | solution.py:86
  202.0 4.8 %while.46 = (s32[]{:T(128)}, f32[48,128,64]{1,0,2:T(8,128)S(1)}, s32[]{:T(128)}, s32[48]{0:T(128)S(1)}, s32[]{:T(128)}, /*index=5*/f32[48,128,128]{2,1,0:T(8,128...) while((s32[]{:T(128)}, f32[48,128,64]{1,0,2:T(8,128)S(1)}, ...), condition=%wide.region_9.12_spmd.clone, body=%wide.region_8.11_spmd.clone.sunk | while | flops 138807088 | bytes 4985255 | solution.py:46
  202.7 2.1 fusion.120
  205.5 1.3 convolution_add_fusion.10
  207.2 12.9 %collective-permute-start.4 = (f32[2048,64]{0,1:T(8,128)S(1)}, f32[2048,64]{0,1:T(8,128)S(1)}, u32[]{:S(2)}, u32[]{:S(2)}) collective-permute-start(f32[2048,64]{0,1:T(8,128)S(1)} %bitcast.148), channel_id=1, source_target_pairs={{0,28},{4,0},{8,4},{12,8},{16,12},{20,16},{24,20},{28,24},{1,29},{... | collective-permute-start | bytes 1572872 | tf_op jit(solution)/shard_map/ppermute | solution.py:11
  220.3 8.9 %collective-permute-start.5 = (f32[2048,64]{0,1:T(8,128)S(1)}, f32[2048,64]{0,1:T(8,128)S(1)}, u32[]{:S(2)}, u32[]{:S(2)}) collective-permute-start(f32[2048,64]{0,1:T(8,128)S(1)} %bitcast.150), channel_id=1, source_target_pairs={{0,4},{4,8},{8,12},{12,16},{16,20},{20,24},{24,28},{28,0},{1,5},{5... | collective-permute-start | bytes 1572872 | tf_op jit(solution)/shard_map/ppermute | solution.py:11
  229.2 12.4 %collective-permute-done.4 = f32[2048,64]{0,1:T(8,128)S(1)} collective-permute-done((f32[2048,64]{0,1:T(8,128)S(1)}, f32[2048,64]{0,1:T(8,128)S(1)}, u32[]{:S(2)}, u32[]{:S(2)}) %collective-permute-start.4) | collective-permute-done | bytes 524320 | tf_op jit(solution)/shard_map/ppermute | solution.py:11
  241.5 3.1 collective-permute-done.5
  244.6 1.0 fusion.57
  245.6 20.9 %reduce-scatter.5.cloned.1.call-done = f32[512,64]{0,1:T(8,128)} async-done(((f32[2048,64]{0,1:T(8,128)}), f32[512,64]{0,1:T(8,128)}) %reduce-scatter.5.cloned.1.call-update) | async-done | bytes 131088 | tf_op jit(solution)/shard_map/reduce_scatter | solution.py:75
  266.6 7.0 %all_gather.7 = f32[2048,64]{0,1:T(8,128)S(1)} all-gather(f32[512,64]{0,1:T(8,128)} %reduce-scatter.5.cloned.1.call-done), channel_id=1, replica_groups=mesh['rows'=8,'grp'=4] {'grp'}, dimensions={0}, use_global_device_ids=true | all-gather | bytes 655360 | tf_op jit(solution)/shard_map/all_gather | solution.py:76
  273.5 1.5 collective-permute-start.6
  275.0 3.2 collective-permute-start.7
  278.3 19.7 %collective-permute-done.6 = f32[2048,64]{0,1:T(8,128)S(1)} collective-permute-done((f32[2048,64]{0,1:T(8,128)S(1)}, f32[2048,64]{0,1:T(8,128)S(1)}, u32[]{:S(2)}, u32[]{:S(2)}) %collective-permute-start.6) | collective-permute-done | bytes 524320 | tf_op jit(solution)/shard_map/ppermute | solution.py:21
  297.9 2.2 collective-permute-done.7
  300.3 2.3 copy.42
  302.5 6.0 %while.47 = (s32[]{:T(128)}, f32[4,128,64]{1,0,2:T(4,128)S(1)}, s32[]{:T(128)}, s32[48]{0:T(128)S(1)}, s32[]{:T(128)}, /*index=5*/f32[48,128,128]{2,1,0:T(8,128)...) while((s32[]{:T(128)}, f32[4,128,64]{1,0,2:T(4,128)S(1)}, ...), condition=%wide.region_12.15_spmd.clone, body=%wide.region_11.14_spmd.clone.sunk | while | flops 103842928 | bytes 2101671 | solution.py:46
  302.7 2.5 gather_fusion.3
  305.1 2.1 fusion.126
  308.8 67.8 %psum.15 = f32[64,64]{0,1:T(8,128)S(1)} all-reduce(f32[64,64]{0,1:T(8,128)S(1)} %convolution_bitcast_fusion.1), channel_id=1, replica_groups=mesh['rows'=8,'grp'=4] {'rows','grp'}, use_global_device_ids=true, to_apply=%region_13.16 | all-reduce | flops 4096 | bytes 32768 | tf_op jit(solution)/shard_map/psum | solution.py:81
  376.7 5.8 %cholesky.55 = f32[64,64]{1,0:T(8,128)S(1)} custom-call(f32[64,64]{1,0:T(8,128)S(1)} %fusion.66), custom_call_target="Cholesky" | custom-call | tf_op jit(solution)/shard_map/jit(cholesky)/cholesky | solution.py:85
  383.9 4.9 %custom-call.7 = f32[1,64,64]{1,2,0:T(8,128)S(1)} custom-call(f32[1,64,64]{2,1,0:T(8,128)S(1)} %fusion.64), custom_call_target="InvertDiagBlocksLowerTriangular" | custom-call | tf_op jit(solution)/shard_map/jit(_solve_triangular)/triangular_solve | solution.py:86
  388.8 1.0 fusion.56
  (48 shorter events, 9.4 us)
Async XLA Ops:
  6.5 72.5 %reduce-scatter.3.cloned.1.call-start = ((), (), s32[]{:S(2)}) async-start(), calls=%async_computation.2 | async-start | bytes 655360 | tf_op jit(solution)/shard_map/reduce_scatter | solution.py:75
  14.9 35.0 %collective-permute-start = (f32[2048,64]{0,1:T(8,128)S(1)}, f32[2048,64]{0,1:T(8,128)S(1)}, u32[]{:S(2)}, u32[]{:S(2)}) collective-permute-start(f32[2048,64]{0,1:T(8,128)S(1)} %bitcast.147), channel_id=1, source_target_pairs={{0,28},{4,0},{8,4},{12,8},{16,12},{20,16},{24,20},{28,24},{1,29},{... | collective-permute-start | bytes 1572872 | tf_op jit(solution)/shard_map/ppermute | solution.py:11
  30.8 24.3 %collective-permute-start.1 = (f32[2048,64]{0,1:T(8,128)S(1)}, f32[2048,64]{0,1:T(8,128)S(1)}, u32[]{:S(2)}, u32[]{:S(2)}) collective-permute-start(f32[2048,64]{0,1:T(8,128)S(1)} %bitcast.149), channel_id=1, source_target_pairs={{0,4},{4,8},{8,12},{12,16},{16,20},{20,24},{24,28},{28,0},{1,5},{5... | collective-permute-start | bytes 1572872 | tf_op jit(solution)/shard_map/ppermute | solution.py:11
  56.1 210.5 %reduce-scatter.5.cloned.1.call-start = ((), (), s32[]{:S(2)}) async-start(), calls=%async_computation.3 | async-start | bytes 655360 | tf_op jit(solution)/shard_map/reduce_scatter | solution.py:75
  86.1 24.4 %collective-permute-start.2 = (f32[2048,64]{0,1:T(8,128)S(1)}, f32[2048,64]{0,1:T(8,128)S(1)}, u32[]{:S(2)}, u32[]{:S(2)}) collective-permute-start(f32[2048,64]{0,1:T(8,128)S(1)} %all_gather.6), channel_id=1, source_target_pairs={{0,4},{4,8},{8,12},{12,16},{16,20},{20,24},{24,28},{28,0},{1,5},{5... | collective-permute-start | bytes 1572872 | tf_op jit(solution)/shard_map/ppermute | solution.py:21
  87.5 25.1 %collective-permute-start.3 = (f32[2048,64]{0,1:T(8,128)S(1)}, f32[2048,64]{0,1:T(8,128)S(1)}, u32[]{:S(2)}, u32[]{:S(2)}) collective-permute-start(f32[2048,64]{0,1:T(8,128)S(1)} %all_gather.6), channel_id=1, source_target_pairs={{4,0},{8,4},{12,8},{16,12},{20,16},{24,20},{28,24},{0,28},{5,1},{9... | collective-permute-start | bytes 1572872 | tf_op jit(solution)/shard_map/ppermute | solution.py:23
  207.2 34.4 %collective-permute-start.4 = (f32[2048,64]{0,1:T(8,128)S(1)}, f32[2048,64]{0,1:T(8,128)S(1)}, u32[]{:S(2)}, u32[]{:S(2)}) collective-permute-start(f32[2048,64]{0,1:T(8,128)S(1)} %bitcast.148), channel_id=1, source_target_pairs={{0,28},{4,0},{8,4},{12,8},{16,12},{20,16},{24,20},{28,24},{1,29},{... | collective-permute-start | bytes 1572872 | tf_op jit(solution)/shard_map/ppermute | solution.py:11
  220.3 24.3 %collective-permute-start.5 = (f32[2048,64]{0,1:T(8,128)S(1)}, f32[2048,64]{0,1:T(8,128)S(1)}, u32[]{:S(2)}, u32[]{:S(2)}) collective-permute-start(f32[2048,64]{0,1:T(8,128)S(1)} %bitcast.150), channel_id=1, source_target_pairs={{0,4},{4,8},{8,12},{12,16},{16,20},{20,24},{24,28},{28,0},{1,5},{5... | collective-permute-start | bytes 1572872 | tf_op jit(solution)/shard_map/ppermute | solution.py:11
  273.5 24.4 %collective-permute-start.6 = (f32[2048,64]{0,1:T(8,128)S(1)}, f32[2048,64]{0,1:T(8,128)S(1)}, u32[]{:S(2)}, u32[]{:S(2)}) collective-permute-start(f32[2048,64]{0,1:T(8,128)S(1)} %all_gather.7), channel_id=1, source_target_pairs={{0,4},{4,8},{8,12},{12,16},{16,20},{20,24},{24,28},{28,0},{1,5},{5... | collective-permute-start | bytes 1572872 | tf_op jit(solution)/shard_map/ppermute | solution.py:21
  275.0 25.1 %collective-permute-start.7 = (f32[2048,64]{0,1:T(8,128)S(1)}, f32[2048,64]{0,1:T(8,128)S(1)}, u32[]{:S(2)}, u32[]{:S(2)}) collective-permute-start(f32[2048,64]{0,1:T(8,128)S(1)} %all_gather.7), channel_id=1, source_target_pairs={{4,0},{8,4},{12,8},{16,12},{20,16},{24,20},{28,24},{0,28},{5,1},{9... | collective-permute-start | bytes 1572872 | tf_op jit(solution)/shard_map/ppermute | solution.py:23
Sparse Core Ops, SparseCore 0:
  56.2 22.8 reduce-scatter.2
  245.7 20.7 reduce-scatter.4
where the time goes:
time: 395 us; the launch traced here: 397 us
  blocking collectives  150 us (38%)
  waiting for transfers between devices  121 us (31%)
  starting transfers between devices  53.7 us (14%)
  other arithmetic  30.9 us (8%)
  between operations  14.3 us (4%)
  matrix products  13.8 us (3%)
  local copies, waits for them, and re-layouts  13.5 us (3%)
    psum x2, blocking collectives, local(): lax.psum(jnp.dot(image.T, image, precision=HIGHEST, preferred_element_typ...  136 us
    ppermute x4, starting transfers between devices, from_behind(): lax.ppermute(array, axis, [(i, (i + by) % peers) for i in range(peers)])  44.2 us
    reduce_scatter x2, waiting for transfers between devices, local(): lax.psum_scatter(summed, 'grp', scatter_dimension=0, tiled=True)  43.9 us
    ppermute x2, waiting for transfers between devices, padded(): lax.ppermute(tail, axis, [(i, (i + 1) % count) for i in range(count)])  39.4 us
    ppermute x4, waiting for transfers between devices, from_behind(): lax.ppermute(array, axis, [(i, (i + by) % peers) for i in range(peers)])  33 us
    all_gather x2, blocking collectives, local(): whole = lax.all_gather(middle_rows, 'grp', axis=0, tiled=True)  14 us
    another operation x6, other arithmetic, local(): lower = jnp.linalg.cholesky(gram)  13.1 us
    another operation x4, other arithmetic, local(): panel = jax.scipy.linalg.solve_triangular(lower, image.T, lower=True).T  11.1 us
  transfers between devices with their start and end apart: 10, of which 10 were waited for; matrix products, arithmetic and copies ran while one was open for 0% of the time, Pallas kernels for 0%

commit v1 on v0

v1 whole, which is shorter than its diff:
```python
import functools

import jax
import jax.numpy as jnp
from jax import lax
from jax.experimental import pallas as pl
from jax.experimental.pallas import tpu as pltpu
from jax.sharding import PartitionSpec as P

HIGHEST = lax.Precision.HIGHEST
MESH = pl.DeviceIdType.MESH
SWEEPS = 2
SUB = 2
UNROLL = 8
PIVOTS = 4


def radices(count):
    found = []
    while count > 1:
        radix = 4 if count % 4 == 0 else next(r for r in range(2, count + 1) if count % r == 0)
        found.append(radix)
        count //= radix
    return found


def dot(a, b):
    return jnp.dot(a, b, precision=HIGHEST, preferred_element_type=jnp.float32)


def dot_nt(a, b, precision=None):
    return lax.dot_general(
        a, b, (((1,), (1,)), ((), ())), precision=precision, preferred_element_type=jnp.float32
    )


def halves(x):
    high = x.astype(jnp.bfloat16)
    low = (x - high.astype(jnp.float32)).astype(jnp.bfloat16)
    return high, low


def inverse_factor(packed, k):
    half = k // 2
    lane = lax.broadcasted_iota(jnp.int32, (half, 2 * k), 1)
    row = lax.broadcasted_iota(jnp.int32, (half, 2 * k), 0)
    one = jnp.float32(1.0)
    zero = jnp.float32(0.0)
    top = jnp.where(lane >= k, pltpu.roll(packed, k, 1), jnp.where(lane == row, one, zero))
    low = jnp.where(lane >= k, packed, jnp.where(lane == row + half, one, zero))
    m = jnp.concatenate([top, low], axis=0)
    rows = lax.broadcasted_iota(jnp.int32, (k, 2 * k), 0)
    pivots = jnp.ones((k, 2 * k), jnp.float32)
    for j in range(0, k, PIVOTS):
        cols = [
            jnp.broadcast_to(m[:, k + j + i : k + j + i + 1], (k, 2 * k)) for i in range(PIVOTS)
        ]
        lines = [m[j + i : j + i + 1, :] for i in range(PIVOTS)]
        for i in range(PIVOTS):
            pivot = cols[i][j + i : j + i + 1, :]
            pivots = jnp.where(rows == j + i, pivot, pivots)
            factor = jnp.where(rows > j + i, cols[i] * (1.0 / pivot), 0.0)
            for n in range(i + 1, PIVOTS):
                lines[n] = lines[n] - factor[j + n : j + n + 1, :] * lines[i]
                cols[n] = cols[n] - factor * cols[i][j + n : j + n + 1, :]
            m = m - factor * lines[i]
    return (m * lax.rsqrt(pivots))[:, :k]


def kernel(
    n_rows, n_grp, total_rows, meta, tiles, sketch, out,
    t2, run, part, rcv1, rcv2, rcv3, spr, img, gbuf, grest, send_sem, recv_sem,
):
    cap, edge, _ = tiles.shape
    tpd, k, _ = img.shape
    half = k // 2
    n_hi = n_grp // 2
    block_tiles = n_grp * tpd
    width = tpd // SUB
    row = lax.axis_index("rows")
    grp = lax.axis_index("grp")
    lo = lax.rem(grp, 2)
    hi = grp // 2
    after = lax.rem(row + 1, n_rows)
    before = lax.rem(row + n_rows - 1, n_rows)
    core_peer = (row, hi * 2 + 1 - lo)

    def hi_peer(step):
        return lax.rem(hi + step, n_hi) * 2 + lo

    near_size = 2 * n_grp
    near_me = lax.rem(row, 2) * n_grp + grp

    def near_peer(step):
        at = lax.rem(near_me + step, near_size)
        return (row // 2 * 2 + at // n_grp, lax.rem(at, n_grp))

    rest = []
    stride = 2
    for radix in radices(n_rows // 2):
        digit = lax.rem(row // stride, radix)
        rest.append((radix, stride, digit))
        stride *= radix

    def rest_peer(stage, step):
        radix, stride, digit = rest[stage]
        return (row + (lax.rem(digit + step, radix) - digit) * stride, grp)

    peers = [(after, grp), (before, grp)]
    peers += [near_peer(s) for s in range(1, near_size)]
    for stage in range(len(rest)):
        peers += [rest_peer(stage, s) for s in range(1, rest[stage][0])]
    barrier = pltpu.get_barrier_semaphore()
    for peer in peers:
        pl.semaphore_signal(barrier, inc=1, device_id=peer, device_id_type=MESH)

    started = []

    def send(src, dst, peer):
        at = len(started)
        copy = pltpu.make_async_remote_copy(
            src_ref=src, dst_ref=dst, send_sem=send_sem.at[at], recv_sem=recv_sem.at[at],
            device_id=peer, device_id_type=MESH,
        )
        copy.start()
        started.append(copy)
        return copy

    def prev_of(s):
        return meta[s]

    def row_of(s):
        return meta[cap + s]

    def col_of(s):
        return meta[2 * cap + s]

    def last_of(t):
        return meta[3 * cap + t]

    run[0] = jnp.zeros((k, edge), jnp.float32)
    for t in range(tpd):
        img[t] = sketch[t * edge : (t + 1) * edge, :].T

    def spread_sweep(first):
        def step(number, carry):
            base = number * UNROLL
            products = []
            for u in range(UNROLL):
                s = base + u
                if first:
                    t_high, t_low = halves(tiles[s])
                    t2[s, 0:edge, :] = t_high
                    t2[s, edge : 2 * edge, :] = t_low
                else:
                    t_high = t2[s, 0:edge, :]
                    t_low = t2[s, edge : 2 * edge, :]
                high, low = halves(img[jnp.maximum(row_of(s), 0)])
                both = jnp.dot(
                    jnp.concatenate([high, low], axis=0), t_high,
                    preferred_element_type=jnp.float32,
                )
                cross = jnp.dot(high, t_low, preferred_element_type=jnp.float32)
                products.append(both[0:k] + (both[k : 2 * k] + cross))
            for u in range(UNROLL):
                s = base + u
                run[s + 1] = products[u] + run[prev_of(s)]
            return carry

        lax.fori_loop(0, cap // UNROLL, step, 0)

    def image_sweep(it):
        for t in range(tpd):
            img[t] = jnp.zeros((k, edge), jnp.float32)

        def step(number, carry):
            base = number * UNROLL
            sums = [None] * tpd
            for u in range(UNROLL):
                s = base + u
                high, low = halves(spr[it, col_of(s)])
                t_high = t2[s, 0:edge, :]
                t_low = t2[s, edge : 2 * edge, :]
                both = dot_nt(jnp.concatenate([high, low], axis=0), t_high)
                cross = dot_nt(high, t_low)
                product = both[0:k] + (both[k : 2 * k] + cross)
                at = row_of(s)
                for t in range(tpd):
                    term = jnp.where(at == t, jnp.float32(1.0), jnp.float32(0.0)) * product
                    sums[t] = term if sums[t] is None else sums[t] + term
            for t in range(tpd):
                img[t] = img[t] + sums[t]
            return carry

        lax.fori_loop(0, cap // UNROLL, step, 0)

    def gram_begin(it):
        total = None
        for t in range(tpd):
            tile = img[t]
            term = dot_nt(tile, jnp.concatenate([tile, tile], axis=0), HIGHEST)
            total = term if total is None else total + term
        lane = lax.broadcasted_iota(jnp.int32, (half, 2 * k), 1)
        gbuf[it, near_me] = jnp.where(lane < k, total[0:half], total[half:k])
        return [
            send(gbuf.at[it, near_me], gbuf.at[it, near_me], near_peer(s))
            for s in range(1, near_size)
        ]

    def gram_near(it, copies):
        for copy in copies:
            copy.wait_recv()
        total = gbuf[it, 0]
        for a in range(1, near_size):
            total = total + gbuf[it, a]
        return total

    def gram_rest_begin(it, stage, total):
        base = sum(r for r, _, _ in rest[:stage])
        radix, _, digit = rest[stage]
        grest[it, base + digit] = total
        return [
            send(grest.at[it, base + digit], grest.at[it, base + digit], rest_peer(stage, s))
            for s in range(1, radix)
        ]

    def gram_rest_end(it, stage, copies):
        base = sum(r for r, _, _ in rest[:stage])
        for copy in copies:
            copy.wait_recv()
        total = grest[it, base]
        for a in range(1, rest[stage][0]):
            total = total + grest[it, base + a]
        return total

    def gram_rest(it, total, copies):
        for stage in range(len(rest)):
            if copies is None:
                copies = gram_rest_begin(it, stage, total)
            total = gram_rest_end(it, stage, copies)
            copies = None
        return total

    def tiles_at(block, g, t=0):
        return block * block_tiles + g * tpd + t

    order = (0, 2, 1)

    def fill(it, block, g):
        def one(t, carry):
            at = tiles_at(block, g) + t
            part[it, at] = run[last_of(at)]
            return carry

        lax.fori_loop(0, tpd, one, 0)

    def scatter_core(it):
        copies = {}
        for block in order:
            for h in range(n_hi):
                g = h * 2 + 1 - lo
                fill(it, block, g)
                copies[block, h] = send(
                    part.at[it, pl.ds(tiles_at(block, g), tpd)],
                    rcv1.at[it, pl.ds((block * n_hi + h) * tpd, tpd)],
                    core_peer,
                )
        for block in order:
            for h in range(n_hi):
                fill(it, block, h * 2 + lo)
        return copies

    def scatter_hi(it, core_copies):
        copies = {}
        for block in order:
            for h in range(n_hi):
                core_copies[block, h].wait_recv()
            for step in range(1, n_hi):
                h = lax.rem(hi + step, n_hi)
                at = tiles_at(block, h * 2 + lo)
                from_core = (block * n_hi + h) * tpd
                for c in range(SUB):
                    mine = pl.ds(at + c * width, width)
                    part[it, mine] = part[it, mine] + rcv1[it, pl.ds(from_core + c * width, width)]
                    slot = (block * (n_hi - 1) + step - 1) * tpd + c * width
                    copies[block, step, c] = send(
                        part.at[it, mine], rcv2.at[it, pl.ds(slot, width)], (row, hi_peer(step))
                    )
        return copies

    def scatter_rows(it, hi_copies):
        copies = []
        for block in order:
            for c in range(SUB):
                mine = pl.ds(tiles_at(block, grp) + c * width, width)
                total = part[it, mine] + rcv1[
                    it, pl.ds((block * n_hi + hi) * tpd + c * width, width)
                ]
                for step in range(1, n_hi):
                    hi_copies[block, step, c].wait_recv()
                    slot = (block * (n_hi - 1) + step - 1) * tpd + c * width
                    total = total + rcv2[it, pl.ds(slot, width)]
                part[it, mine] = total
                if block == 0:
                    copies.append(
                        send(part.at[it, mine], rcv3.at[it, pl.ds(c * width, width)], (before, grp))
                    )
                if block == 2:
                    copies.append(
                        send(
                            part.at[it, mine],
                            rcv3.at[it, pl.ds(tpd + c * width, width)],
                            (after, grp),
                        )
                    )
        return copies

    def gather(it, row_copies, inverse):
        lead = []
        for c in range(SUB):
            row_copies[c].wait_recv()
            row_copies[SUB + c].wait_recv()
            for w in range(width):
                t = c * width + w
                value = part[it, tiles_at(1, grp) + t] + (rcv3[it, t] + rcv3[it, tpd + t])
                if inverse is not None:
                    value = dot(inverse, value)
                spr[it, tiles_at(1, grp) + t] = value

            def at(block, g, c=c):
                return spr.at[it, pl.ds(tiles_at(block, g) + c * width, width)]

            own = at(1, grp)
            up = send(own, at(0, grp), (after, grp))
            down = send(own, at(2, grp), (before, grp))
            across = [send(own, at(1, grp), (row, hi_peer(s))) for s in range(1, n_hi)]
            core = send(own, at(1, grp), core_peer)
            lead.append((up, down, across, core, at))
        last = []
        later = []
        for up, down, across, core, at in lead:
            last.append(core)
            for block, copy in ((0, up), (2, down)):
                copy.wait_recv()
                piece = at(block, grp)
                for s in range(1, n_hi):
                    later.append((block, s, at, send(piece, piece, (row, hi_peer(s)))))
                last.append(send(piece, piece, core_peer))
            for s in range(1, n_hi):
                across[s - 1].wait_recv()
                piece = at(1, hi_peer(n_hi - s))
                last.append(send(piece, piece, core_peer))
        for block, s, at, copy in later:
            copy.wait_recv()
            piece = at(block, hi_peer(n_hi - s))
            last.append(send(piece, piece, core_peer))
        for copy in last:
            copy.wait_recv()

    inverse = None
    near = None
    for it in range(SWEEPS):
        spread_sweep(it == 0)
        if it == 0:
            pl.semaphore_wait(barrier, len(peers))
        core_copies = scatter_core(it)
        far = None
        if near is not None:
            total = gram_near(it - 1, near)
            if rest:
                far = gram_rest_begin(it - 1, 0, total)
        hi_copies = scatter_hi(it, core_copies)
        row_copies = scatter_rows(it, hi_copies)
        if near is not None:
            inverse = inverse_factor(gram_rest(it - 1, total, far), k)
        gather(it, row_copies, inverse)
        image_sweep(it)
        near = gram_begin(it)
    total = gram_rest(SWEEPS - 1, gram_near(SWEEPS - 1, near), None)
    inverse = inverse_factor(total, k) * jnp.float32(total_rows**0.5)
    for t in range(tpd):
        out[:, t * edge : (t + 1) * edge] = dot(inverse, img[t])
    for copy in started:
        copy.wait_send()


def copies_of(n_rows, n_grp):
    n_hi = n_grp // 2
    scatter = 3 * n_hi + 3 * (n_hi - 1) * SUB + 2 * SUB
    gather = SUB * (2 + (n_hi - 1) + 1 + 2 * n_hi + 3 * (n_hi - 1))
    gram = 2 * n_grp - 1 + sum(r - 1 for r in radices(n_rows // 2))
    return SWEEPS * (scatter + gather + gram)


def local(tiles, coords, live, sketch):
    n_grp = lax.axis_size("grp")
    n_rows = lax.axis_size("rows")
    row = lax.axis_index("rows")
    grp = lax.axis_index("grp")
    cap, edge, _ = tiles.shape
    k = sketch.shape[1]
    tpd = sketch.shape[0] // edge
    block_tiles = n_grp * tpd
    targets = 3 * block_tiles
    slots = jnp.arange(cap, dtype=jnp.int32)
    used = slots < live[0]
    row_pos = coords[:, 0] - (row * block_tiles + grp * tpd)
    col_tiles = coords[:, 1]
    col_pos = (
        (col_tiles // block_tiles - row + 1 + n_rows) % n_rows * block_tiles
        + col_tiles % block_tiles
    )
    wanted = jnp.concatenate([col_pos, jnp.arange(targets, dtype=jnp.int32)])
    until = jnp.concatenate([slots, jnp.full((targets,), cap, jnp.int32)])
    same = (wanted[:, None] == col_pos[None, :]) & used[None, :] & (slots[None, :] < until[:, None])
    link = jnp.max(jnp.where(same, slots[None, :] + 1, 0), axis=1)
    meta = jnp.concatenate(
        [
            link[:cap],
            jnp.where(used, row_pos, -1),
            jnp.clip(col_pos, 0, targets - 1),
            link[cap:],
        ]
    )
    n_hi = n_grp // 2
    n_copies = copies_of(n_rows, n_grp)
    f32 = jnp.float32
    vmem = pl.BlockSpec(memory_space=pltpu.VMEM)
    basis = pl.pallas_call(
        functools.partial(kernel, n_rows, n_grp, n_rows * n_grp * sketch.shape[0]),
        out_shape=jax.ShapeDtypeStruct((k, tpd * edge), f32),
        in_specs=[pl.BlockSpec(memory_space=pltpu.SMEM), vmem, vmem],
        out_specs=vmem,
        scratch_shapes=[
            pltpu.VMEM((cap, 2 * edge, edge), jnp.bfloat16),
            pltpu.VMEM((cap + 1, k, edge), f32),
            pltpu.VMEM((SWEEPS, targets, k, edge), f32),
            pltpu.VMEM((SWEEPS, 3 * n_hi * tpd, k, edge), f32),
            pltpu.VMEM((SWEEPS, 3 * max(n_hi - 1, 1) * tpd, k, edge), f32),
            pltpu.VMEM((SWEEPS, 2 * tpd, k, edge), f32),
            pltpu.VMEM((SWEEPS, targets, k, edge), f32),
            pltpu.VMEM((tpd, k, edge), f32),
            pltpu.VMEM((SWEEPS, 2 * n_grp, k // 2, 2 * k), f32),
            pltpu.VMEM((SWEEPS, max(sum(radices(n_rows // 2)), 1), k // 2, 2 * k), f32),
            pltpu.SemaphoreType.DMA((n_copies,)),
            pltpu.SemaphoreType.DMA((n_copies,)),
        ],
        compiler_params=pltpu.CompilerParams(
            collective_id=0, has_side_effects=True, vmem_limit_bytes=48 * 1024 * 1024
        ),
    )(meta, tiles, sketch)
    return basis.T


def solution(mesh):
    return jax.shard_map(
        local,
        mesh=mesh,
        in_specs=(
            P(("rows", "grp"), None, None),
            P(("rows", "grp"), None),
            P(("rows", "grp")),
            P(("rows", "grp"), None),
        ),
        out_specs=P(("rows", "grp"), None),
        check_vma=False,
    )
```

time: 395 us -> 87 us (0.22)
  blocking collectives: 150 us -> 0 us
  waiting for transfers between devices: 121 us -> 0 us
  Pallas kernels: 0 us -> 80.7 us
  starting transfers between devices: 53.7 us -> 0 us
  other arithmetic: 30.9 us -> 1.7 us
  matrix products: 13.8 us -> 0 us
  between operations: 14.3 us -> 0.7 us
  local copies, waits for them, and re-layouts: 13.5 us -> 3.65 us
    psum x2 -> x0, blocking collectives: 136 us -> none  [local(): lax.psum(jnp.dot(image.T, image, precision=HIGHEST, preferred_element_typ...]
    pallas_call x0 -> x1, Pallas kernels: none -> 80.7 us  [local(): pl.pallas_call(functools.partial(kernel, n_rows, n_grp, n_rows * n_grp *...]
    ppermute x8 -> x0, waiting for transfers between devices: 76.8 us -> none  [the longest x2 39.4 us: padded(): lax.ppermute(tail, axis, [(i, (i + 1) % count) for i in range(count)])]
    ppermute x8 -> x0, starting transfers between devices: 53.6 us -> none  [the longest x4 44.2 us: from_behind(): lax.ppermute(array, axis, [(i, (i + by) % peers) for i in range(peers)])]
    reduce_scatter x2 -> x0, waiting for transfers between devices: 43.9 us -> none  [local(): lax.psum_scatter(summed, 'grp', scatter_dimension=0, tiled=True)]
    another operation x10 -> x0, other arithmetic: 24.3 us -> none  [the longest x6 13.1 us: local(): lower = jnp.linalg.cholesky(gram)]
    all_gather x2 -> x0, blocking collectives: 14 us -> none  [local(): whole = lax.all_gather(middle_rows, 'grp', axis=0, tiled=True)]
    dot_general x10 -> x0, matrix products: 12.5 us -> none  [the longest x4 8.36 us: advance(): product = jnp.einsum(pattern, stacked, source[fetched], precision=HIGHEST)]
  transfers between devices with their start and end apart: 10 -> 0, of which waited for: 10 -> 0; matrix products, arithmetic and copies ran while one was open for 0% -> 0% of each run, Pallas kernels for 0% -> 0%
where the time goes in v1:
time: 87 us; the launch traced here: 86.8 us
  Pallas kernels  80.7 us (93%)
  local copies, waits for them, and re-layouts  3.65 us (4%)
  other arithmetic  1.7 us (2%)
    pallas_call x1, Pallas kernels, local(): pl.pallas_call(functools.partial(kernel, n_rows, n_grp, n_rows * n_grp *...  80.7 us
    unnamed x4, local copies, waits for them, and re-layouts  3.58 us

profile of v1, /device:TPU:0, one launch (start us, length us, event | category | flops | bytes accessed | tf_op | source)
XLA Modules:
  0.0 86.8 jit_solution(10039501933285551341)
XLA Ops:
  0.7 0.8 broadcast_clamp_fusion
  1.5 0.1 pad_add_fusion.1
  1.5 0.8 select_reduce_fusion
  2.3 0.1 fusion.5
  2.4 0.1 pad_add_fusion.meta
  2.4 1.0 %copy.6.sketch = f32[512,64]{1,0:T(8,128)S(1)} copy(f32[512,64]{0,1:T(8,128)} %param.7) | data formatting | bytes 262144 | tf_op args[3]
  3.5 0.0 copy-start
  3.5 1.9 %copy-done = f32[48,128,128]{2,1,0:T(8,128)S(1)} copy-done((f32[48,128,128]{2,1,0:T(8,128)S(1)}, f32[48,128,128]{2,1,0:T(8,128)}, u32[]{:S(2)}) %copy-start) | copy-done | bytes 3145752
  5.4 80.7 %shard_map.46 = f32[64,512]{1,0:T(8,128)S(1)} custom-call(s32[192]{0:T(256)S(1)} %pad_add_fusion.meta, f32[48,128,128]{2,1,0:T(8,128)S(1)} %copy-done, f32[512,64]{1,0:T(8,128)S(1)} %copy.6.sketch), custom_call_target="tpu_custom_call" | custom-call | tf_op jit(solution)/shard_map/pallas_call | solution.py:429
  86.1 0.7 copy.9
  (2 shorter events, 0.0 us)
Async XLA Ops:
  3.5 1.9 %copy-start = (f32[48,128,128]{2,1,0:T(8,128)S(1)}, f32[48,128,128]{2,1,0:T(8,128)}, u32[]{:S(2)}) copy-start(f32[48,128,128]{2,1,0:T(8,128)} %tiles.1) | copy-start | bytes 9437188

commit v2 on v1

--- a/solution.py
+++ b/solution.py
@@ -10,7 +10,7 @@
 HIGHEST = lax.Precision.HIGHEST
 MESH = pl.DeviceIdType.MESH
 SWEEPS = 2
-SUB = 2
+SUB = 4
 UNROLL = 8
 PIVOTS = 4
 
@@ -40,7 +40,7 @@
     return high, low
 
 
-def inverse_factor(packed, k):
+def augmented(packed, k):
     half = k // 2
     lane = lax.broadcasted_iota(jnp.int32, (half, 2 * k), 1)
     row = lax.broadcasted_iota(jnp.int32, (half, 2 * k), 0)
@@ -48,10 +48,13 @@
     zero = jnp.float32(0.0)
     top = jnp.where(lane >= k, pltpu.roll(packed, k, 1), jnp.where(lane == row, one, zero))
     low = jnp.where(lane >= k, packed, jnp.where(lane == row + half, one, zero))
-    m = jnp.concatenate([top, low], axis=0)
+    return jnp.concatenate([top, low], axis=0), jnp.ones((k, 2 * k), jnp.float32)
+
+
+def eliminate(state, k, columns):
+    m, pivots = state
     rows = lax.broadcasted_iota(jnp.int32, (k, 2 * k), 0)
-    pivots = jnp.ones((k, 2 * k), jnp.float32)
-    for j in range(0, k, PIVOTS):
+    for j in columns:
         cols = [
             jnp.broadcast_to(m[:, k + j + i : k + j + i + 1], (k, 2 * k)) for i in range(PIVOTS)
         ]
@@ -64,12 +67,17 @@
                 lines[n] = lines[n] - factor[j + n : j + n + 1, :] * lines[i]
                 cols[n] = cols[n] - factor * cols[i][j + n : j + n + 1, :]
             m = m - factor * lines[i]
+    return m, pivots
+
+
+def inverse_of(state, k):
+    m, pivots = state
     return (m * lax.rsqrt(pivots))[:, :k]
 
 
 def kernel(
-    n_rows, n_grp, total_rows, meta, tiles, sketch, out,
-    t2, run, part, rcv1, rcv2, rcv3, spr, img, gbuf, grest, send_sem, recv_sem,
+    n_rows, n_grp, total_rows, meta, stored, sketch, out,
+    tiles, t2, run, part, rcv1, rcv2, rcv3, spr, img, gbuf, grest, load_sem, send_sem, recv_sem,
 ):
     cap, edge, _ = tiles.shape
     tpd, k, _ = img.shape
@@ -106,6 +114,13 @@
         radix, stride, digit = rest[stage]
         return (row + (lax.rem(digit + step, radix) - digit) * stride, grp)
 
+    def load(number):
+        some = pl.ds(number * UNROLL, UNROLL)
+        return pltpu.make_async_copy(stored.at[some], tiles.at[some], load_sem.at[number])
+
+    for number in range(cap // UNROLL):
+        load(number).start()
+
     peers = [(after, grp), (before, grp)]
     peers += [near_peer(s) for s in range(1, near_size)]
     for stage in range(len(rest)):
@@ -140,12 +155,14 @@
 
     run[0] = jnp.zeros((k, edge), jnp.float32)
     for t in range(tpd):
-        img[t] = sketch[t * edge : (t + 1) * edge, :].T
+        img[t] = sketch[:, t * edge : (t + 1) * edge]
 
     def spread_sweep(first):
         def step(number, carry):
             base = number * UNROLL
             products = []
+            if first:
+                load(number).wait()
             for u in range(UNROLL):
                 s = base + u
                 if first:
@@ -288,9 +305,9 @@
                     )
         return copies
 
-    def scatter_rows(it, hi_copies):
+    def scatter_rows(it, hi_copies, blocks):
         copies = []
-        for block in order:
+        for block in blocks:
             for c in range(SUB):
                 mine = pl.ds(tiles_at(block, grp) + c * width, width)
                 total = part[it, mine] + rcv1[
@@ -370,14 +387,19 @@
             if rest:
                 far = gram_rest_begin(it - 1, 0, total)
         hi_copies = scatter_hi(it, core_copies)
-        row_copies = scatter_rows(it, hi_copies)
         if near is not None:
-            inverse = inverse_factor(gram_rest(it - 1, total, far), k)
+            state = augmented(gram_rest(it - 1, total, far), k)
+            state = eliminate(state, k, range(0, k // 2, PIVOTS))
+        row_copies = scatter_rows(it, hi_copies, order[:2])
+        if near is not None:
+            inverse = inverse_of(eliminate(state, k, range(k // 2, k, PIVOTS)), k)
+        scatter_rows(it, hi_copies, order[2:])
         gather(it, row_copies, inverse)
         image_sweep(it)
         near = gram_begin(it)
     total = gram_rest(SWEEPS - 1, gram_near(SWEEPS - 1, near), None)
-    inverse = inverse_factor(total, k) * jnp.float32(total_rows**0.5)
+    state = eliminate(augmented(total, k), k, range(0, k, PIVOTS))
+    inverse = inverse_of(state, k) * jnp.float32(total_rows**0.5)
     for t in range(tpd):
         out[:, t * edge : (t + 1) * edge] = dot(inverse, img[t])
     for copy in started:
@@ -429,9 +451,12 @@
     basis = pl.pallas_call(
         functools.partial(kernel, n_rows, n_grp, n_rows * n_grp * sketch.shape[0]),
         out_shape=jax.ShapeDtypeStruct((k, tpd * edge), f32),
-        in_specs=[pl.BlockSpec(memory_space=pltpu.SMEM), vmem, vmem],
+        in_specs=[
+            pl.BlockSpec(memory_space=pltpu.SMEM), pl.BlockSpec(memory_space=pltpu.HBM), vmem,
+        ],
         out_specs=vmem,
         scratch_shapes=[
+            pltpu.VMEM((cap, edge, edge), f32),
             pltpu.VMEM((cap, 2 * edge, edge), jnp.bfloat16),
             pltpu.VMEM((cap + 1, k, edge), f32),
             pltpu.VMEM((SWEEPS, targets, k, edge), f32),
@@ -442,13 +467,14 @@
             pltpu.VMEM((tpd, k, edge), f32),
             pltpu.VMEM((SWEEPS, 2 * n_grp, k // 2, 2 * k), f32),
             pltpu.VMEM((SWEEPS, max(sum(radices(n_rows // 2)), 1), k // 2, 2 * k), f32),
+            pltpu.SemaphoreType.DMA((cap // UNROLL,)),
             pltpu.SemaphoreType.DMA((n_copies,)),
             pltpu.SemaphoreType.DMA((n_copies,)),
         ],
         compiler_params=pltpu.CompilerParams(
             collective_id=0, has_side_effects=True, vmem_limit_bytes=48 * 1024 * 1024
         ),
-    )(meta, tiles, sketch)
+    )(meta, tiles, sketch.T)
     return basis.T
 
 

time: 87 us -> 84.1 us (0.967)
  Pallas kernels: 80.7 us -> 78 us
    pallas_call x1, Pallas kernels: 80.7 us -> 78 us  [local(): pl.pallas_call(functools.partial(kernel, n_rows, n_grp, n_rows * n_grp *...]
    unnamed x4 -> x5, local copies, waits for them, and re-layouts: 3.58 us -> 3.46 us
where the time goes in v2:
time: 84.1 us; the launch traced here: 83.9 us
  Pallas kernels  78 us (93%)
  local copies, waits for them, and re-layouts  3.53 us (4%)
  other arithmetic  1.7 us (2%)
    pallas_call x1, Pallas kernels, local(): pl.pallas_call(functools.partial(kernel, n_rows, n_grp, n_rows * n_grp *...  78 us
    unnamed x5, local copies, waits for them, and re-layouts  3.46 us

profile of v2, /device:TPU:0, one launch (start us, length us, event | category | flops | bytes accessed | tf_op | source)
XLA Modules:
  0.0 83.9 jit_solution(647046462702082352)
XLA Ops:
  0.7 0.8 broadcast_clamp_fusion
  1.5 0.1 pad_add_fusion.1
  1.5 0.8 select_reduce_fusion
  2.3 0.1 fusion.5
  2.4 0.1 pad_add_fusion.meta
  2.4 0.0 copy-start
  2.4 1.9 %copy-done = f32[48,128,128]{2,1,0:T(8,128)S(1)} copy-done((f32[48,128,128]{2,1,0:T(8,128)S(1)}, f32[48,128,128]{2,1,0:T(8,128)}, u32[]{:S(2)}) %copy-start) | copy-done | bytes 3145752
  4.3 0.0 copy-start.1
  4.3 0.9 %copy-done.1 = f32[512,64]{0,1:T(8,128)S(1)} copy-done((f32[512,64]{0,1:T(8,128)S(1)}, f32[512,64]{0,1:T(8,128)}, u32[]{:S(2)}) %copy-start.1) | copy-done | bytes 131096
  5.2 78.0 %shard_map.46 = f32[64,512]{1,0:T(8,128)S(1)} custom-call(s32[192]{0:T(256)S(1)} %pad_add_fusion.meta, f32[48,128,128]{2,1,0:T(8,128)S(1)} %copy-done, f32[64,512]{1,0:T(8,128)S(1)} %bitcast.22), custom_call_target="tpu_custom_call" | custom-call | tf_op jit(solution)/shard_map/pallas_call | solution.py:451
  83.2 0.7 copy.7
  (2 shorter events, 0.0 us)
Async XLA Ops:
  2.4 1.9 %copy-start = (f32[48,128,128]{2,1,0:T(8,128)S(1)}, f32[48,128,128]{2,1,0:T(8,128)}, u32[]{:S(2)}) copy-start(f32[48,128,128]{2,1,0:T(8,128)} %stored.1) | copy-start | bytes 9437188
  4.3 0.9 %copy-start.1 = (f32[512,64]{0,1:T(8,128)S(1)}, f32[512,64]{0,1:T(8,128)}, u32[]{:S(2)}) copy-start(f32[512,64]{0,1:T(8,128)} %param.7) | copy-start | bytes 393220

commit v3 on v2

--- a/solution.py
+++ b/solution.py
@@ -38,6 +38,13 @@
     high = x.astype(jnp.bfloat16)
     low = (x - high.astype(jnp.float32)).astype(jnp.bfloat16)
     return high, low
+
+
+def quarters(x):
+    rows, columns = x.shape[0] // 2, x.shape[1] // 2
+    return x[:rows, :columns] + (
+        (x[rows:, :columns] + x[:rows, columns:]) + x[rows:, columns:]
+    )
 
 
 def augmented(packed, k):
@@ -77,7 +84,7 @@
 
 def kernel(
     n_rows, n_grp, total_rows, meta, stored, sketch, out,
-    tiles, t2, run, part, rcv1, rcv2, rcv3, spr, img, gbuf, grest, load_sem, send_sem, recv_sem,
+    tiles, t2, t3, run, part, rcv1, rcv2, rcv3, spr, img, gbuf, grest, load_sem, send_sem, recv_sem,
 ):
     cap, edge, _ = tiles.shape
     tpd, k, _ = img.shape
@@ -169,16 +176,19 @@
                     t_high, t_low = halves(tiles[s])
                     t2[s, 0:edge, :] = t_high
                     t2[s, edge : 2 * edge, :] = t_low
+                    wide = jnp.concatenate([t_high, t_low], axis=1)
+                    t3[s] = wide
                 else:
-                    t_high = t2[s, 0:edge, :]
-                    t_low = t2[s, edge : 2 * edge, :]
+                    wide = t3[s]
                 high, low = halves(img[jnp.maximum(row_of(s), 0)])
-                both = jnp.dot(
-                    jnp.concatenate([high, low], axis=0), t_high,
-                    preferred_element_type=jnp.float32,
+                products.append(
+                    quarters(
+                        jnp.dot(
+                            jnp.concatenate([high, low], axis=0), wide,
+                            preferred_element_type=jnp.float32,
+                        )
+                    )
                 )
-                cross = jnp.dot(high, t_low, preferred_element_type=jnp.float32)
-                products.append(both[0:k] + (both[k : 2 * k] + cross))
             for u in range(UNROLL):
                 s = base + u
                 run[s + 1] = products[u] + run[prev_of(s)]
@@ -196,11 +206,7 @@
             for u in range(UNROLL):
                 s = base + u
                 high, low = halves(spr[it, col_of(s)])
-                t_high = t2[s, 0:edge, :]
-                t_low = t2[s, edge : 2 * edge, :]
-                both = dot_nt(jnp.concatenate([high, low], axis=0), t_high)
-                cross = dot_nt(high, t_low)
-                product = both[0:k] + (both[k : 2 * k] + cross)
+                product = quarters(dot_nt(jnp.concatenate([high, low], axis=0), t2[s]))
                 at = row_of(s)
                 for t in range(tpd):
                     term = jnp.where(at == t, jnp.float32(1.0), jnp.float32(0.0)) * product
@@ -458,6 +464,7 @@
         scratch_shapes=[
             pltpu.VMEM((cap, edge, edge), f32),
             pltpu.VMEM((cap, 2 * edge, edge), jnp.bfloat16),
+            pltpu.VMEM((cap, edge, 2 * edge), jnp.bfloat16),
             pltpu.VMEM((cap + 1, k, edge), f32),
             pltpu.VMEM((SWEEPS, targets, k, edge), f32),
             pltpu.VMEM((SWEEPS, 3 * n_hi * tpd, k, edge), f32),
@@ -472,7 +479,7 @@
             pltpu.SemaphoreType.DMA((n_copies,)),
         ],
         compiler_params=pltpu.CompilerParams(
-            collective_id=0, has_side_effects=True, vmem_limit_bytes=48 * 1024 * 1024
+            collective_id=0, has_side_effects=True, vmem_limit_bytes=62 * 1024 * 1024
         ),
     )(meta, tiles, sketch.T)
     return basis.T

time: 84.1 us -> 82.8 us (0.985)
  local copies, waits for them, and re-layouts: 3.53 us -> 1.64 us
    unnamed x5 -> x1, local copies, waits for them, and re-layouts: 3.46 us -> 1.57 us
where the time goes in v3:
time: 82.8 us; the launch traced here: 82.6 us
  Pallas kernels  78 us (94%)
  other arithmetic  2.26 us (3%)
  local copies, waits for them, and re-layouts  1.64 us (2%)
    pallas_call x1, Pallas kernels, local(): pl.pallas_call(functools.partial(kernel, n_rows, n_grp, n_rows * n_grp *...  78 us

profile of v3, /device:TPU:0, one launch (start us, length us, event | category | flops | bytes accessed | tf_op | source)
XLA Modules:
  0.0 82.6 jit_solution(17823893086173855360)
XLA Ops:
  0.7 0.8 broadcast_clamp_fusion
  1.5 0.1 pad_add_fusion.1
  1.5 0.8 select_reduce_fusion
  2.3 0.1 fusion.5
  2.4 0.6 pad_add_fusion.meta
  3.0 78.0 %shard_map.46 = f32[64,512]{1,0:T(8,128)} custom-call(s32[192]{0:T(256)} %pad_add_fusion.meta, f32[48,128,128]{2,1,0:T(8,128)} %stored.1, f32[64,512]{1,0:T(8,128)} %bitcast.22), custom_call_target="tpu_custom_call" | custom-call | tf_op jit(solution)/shard_map/pallas_call | solution.py:457
  81.0 1.6 %copy.7 = f32[512,64]{0,1:T(8,128)} copy(f32[512,64]{0,1:T(8,128)} %bitcast.21) | data formatting | bytes 262144
  (2 shorter events, 0.0 us)

commit v4 on v3

--- a/solution.py
+++ b/solution.py
@@ -302,14 +302,34 @@
                 h = lax.rem(hi + step, n_hi)
                 at = tiles_at(block, h * 2 + lo)
                 from_core = (block * n_hi + h) * tpd
-                for c in range(SUB):
+                for c in range(SUB - 1, -1, -1):
+                    if (block, c) == (1, 0):
+                        continue
                     mine = pl.ds(at + c * width, width)
                     part[it, mine] = part[it, mine] + rcv1[it, pl.ds(from_core + c * width, width)]
                     slot = (block * (n_hi - 1) + step - 1) * tpd + c * width
+                    peer = (row, hi_peer(step))
+                    if c == 0:
+                        peer = (before if block == 0 else after, grp)
                     copies[block, step, c] = send(
-                        part.at[it, mine], rcv2.at[it, pl.ds(slot, width)], (row, hi_peer(step))
+                        part.at[it, mine], rcv2.at[it, pl.ds(slot, width)], peer
                     )
         return copies
+
+    def scatter_late(it, copies):
+        for step in range(1, n_hi):
+            h = lax.rem(hi + step, n_hi)
+            mine = pl.ds(tiles_at(1, h * 2 + lo), width)
+            total = part[it, mine] + rcv1[it, pl.ds((n_hi + h) * tpd, width)]
+            for block in (0, 2):
+                copies[block, step, 0].wait_recv()
+                slot = (block * (n_hi - 1) + step - 1) * tpd
+                total = total + rcv2[it, pl.ds(slot, width)]
+            part[it, mine] = total
+            slot = (n_hi - 1 + step - 1) * tpd
+            copies[1, step, 0] = send(
+                part.at[it, mine], rcv2.at[it, pl.ds(slot, width)], (row, hi_peer(step))
+            )
 
     def scatter_rows(it, hi_copies, blocks):
         copies = []
@@ -320,6 +340,8 @@
                     it, pl.ds((block * n_hi + hi) * tpd + c * width, width)
                 ]
                 for step in range(1, n_hi):
+                    if block != 1 and c == 0:
+                        continue
                     hi_copies[block, step, c].wait_recv()
                     slot = (block * (n_hi - 1) + step - 1) * tpd + c * width
                     total = total + rcv2[it, pl.ds(slot, width)]
@@ -358,20 +380,24 @@
             down = send(own, at(2, grp), (before, grp))
             across = [send(own, at(1, grp), (row, hi_peer(s))) for s in range(1, n_hi)]
             core = send(own, at(1, grp), core_peer)
-            lead.append((up, down, across, core, at))
+            lead.append((up, down, across, core, at, c == 0))
         last = []
         later = []
-        for up, down, across, core, at in lead:
+        for up, down, across, core, at, first in lead:
             last.append(core)
             for block, copy in ((0, up), (2, down)):
                 copy.wait_recv()
                 piece = at(block, grp)
-                for s in range(1, n_hi):
+                for s in range(1, 1 if first else n_hi):
                     later.append((block, s, at, send(piece, piece, (row, hi_peer(s)))))
                 last.append(send(piece, piece, core_peer))
             for s in range(1, n_hi):
                 across[s - 1].wait_recv()
-                piece = at(1, hi_peer(n_hi - s))
+                source = hi_peer(n_hi - s)
+                piece = at(1, source)
+                if first:
+                    later.append((0, s, at, send(piece, at(0, source), (after, grp))))
+                    later.append((2, s, at, send(piece, at(2, source), (before, grp))))
                 last.append(send(piece, piece, core_peer))
         for block, s, at, copy in later:
             copy.wait_recv()
@@ -397,6 +423,7 @@
             state = augmented(gram_rest(it - 1, total, far), k)
             state = eliminate(state, k, range(0, k // 2, PIVOTS))
         row_copies = scatter_rows(it, hi_copies, order[:2])
+        scatter_late(it, hi_copies)
         if near is not None:
             inverse = inverse_of(eliminate(state, k, range(k // 2, k, PIVOTS)), k)
         scatter_rows(it, hi_copies, order[2:])
@@ -479,7 +506,7 @@
             pltpu.SemaphoreType.DMA((n_copies,)),
         ],
         compiler_params=pltpu.CompilerParams(
-            collective_id=0, has_side_effects=True, vmem_limit_bytes=62 * 1024 * 1024
+            collective_id=0, has_side_effects=True, vmem_limit_bytes=245 * 256 * 1024
         ),
     )(meta, tiles, sketch.T)
     return basis.T

time: 82.8 us -> 82.2 us (level)
  no operation moved by 1% of the time
where the time goes in v4:
time: 82.2 us; the launch traced here: 82 us
  Pallas kernels  77.4 us (94%)
  other arithmetic  2.26 us (3%)
  local copies, waits for them, and re-layouts  1.64 us (2%)
    pallas_call x1, Pallas kernels, local(): pl.pallas_call(functools.partial(kernel, n_rows, n_grp, n_rows * n_grp *...  77.4 us

profile of v4, /device:TPU:0, one launch (start us, length us, event | category | flops | bytes accessed | tf_op | source)
XLA Modules:
  0.0 82.0 jit_solution(7698511152979752368)
XLA Ops:
  0.7 0.8 broadcast_clamp_fusion
  1.5 0.1 pad_add_fusion.1
  1.5 0.8 select_reduce_fusion
  2.3 0.1 fusion.5
  2.4 0.6 pad_add_fusion.meta
  3.0 77.4 %shard_map.46 = f32[64,512]{1,0:T(8,128)} custom-call(s32[192]{0:T(256)} %pad_add_fusion.meta, f32[48,128,128]{2,1,0:T(8,128)} %stored.1, f32[64,512]{1,0:T(8,128)} %bitcast.22), custom_call_target="tpu_custom_call" | custom-call | tf_op jit(solution)/shard_map/pallas_call | solution.py:484
  80.4 1.6 %copy.7 = f32[512,64]{0,1:T(8,128)} copy(f32[512,64]{0,1:T(8,128)} %bitcast.21) | data formatting | bytes 262144
  (2 shorter events, 0.0 us)

commit v5 on v4

--- a/solution.py
+++ b/solution.py
@@ -12,7 +12,7 @@
 SWEEPS = 2
 SUB = 4
 UNROLL = 8
-PIVOTS = 4
+PIVOTS = 8
 
 
 def radices(count):

time: 82.2 us -> 80.5 us (0.979)
  Pallas kernels: 77.4 us -> 75.7 us
    pallas_call x1, Pallas kernels: 77.4 us -> 75.7 us  [local(): pl.pallas_call(functools.partial(kernel, n_rows, n_grp, n_rows * n_grp *...]
where the time goes in v5:
time: 80.5 us; the launch traced here: 80.3 us
  Pallas kernels  75.7 us (94%)
  other arithmetic  2.26 us (3%)
  local copies, waits for them, and re-layouts  1.64 us (2%)
    pallas_call x1, Pallas kernels, local(): pl.pallas_call(functools.partial(kernel, n_rows, n_grp, n_rows * n_grp *...  75.7 us

profile of v5, /device:TPU:0, one launch (start us, length us, event | category | flops | bytes accessed | tf_op | source)
XLA Modules:
  0.0 80.3 jit_solution(5787455760917138051)
XLA Ops:
  0.7 0.8 broadcast_clamp_fusion
  1.5 0.1 pad_add_fusion.1
  1.5 0.8 select_reduce_fusion
  2.3 0.1 fusion.5
  2.4 0.6 pad_add_fusion.meta
  3.0 75.7 %shard_map.46 = f32[64,512]{1,0:T(8,128)} custom-call(s32[192]{0:T(256)} %pad_add_fusion.meta, f32[48,128,128]{2,1,0:T(8,128)} %stored.1, f32[64,512]{1,0:T(8,128)} %bitcast.22), custom_call_target="tpu_custom_call" | custom-call | tf_op jit(solution)/shard_map/pallas_call | solution.py:484
  78.7 1.6 %copy.7 = f32[512,64]{0,1:T(8,128)} copy(f32[512,64]{0,1:T(8,128)} %bitcast.21) | data formatting | bytes 262144
  (2 shorter events, 0.0 us)
